TPU v7x, 32 devices: a whole 2x2x4 slice. The times are simulated.
32 devices in a mesh: groups: 2 (over y), seq: 8 (over z, x), head: 2 (over core).
Axes of the slice: x: 2, y: 2, z: 4, core: 2. Of those that a mesh axis runs over, the one named last changes fastest.
Arguments:
- queries: bfloat16 [2048, 768], P(('groups', 'seq'), 'head'), parts along dimension 0, may hold values from -6.5 to 6.5
- key_rows: bfloat16 [2048, 768], P(('groups', 'seq'), 'head'), parts along dimension 0, may hold values from -6.5 to 6.5
- value_rows: bfloat16 [2048, 768], P(('groups', 'seq'), 'head'), parts along dimension 0, may hold values from -6 to 6
- grad_out: bfloat16 [2048, 768], P(('groups', 'seq'), 'head'), parts along dimension 0, may hold values from -6 to 6
- offsets: int32 [8, 16], replicated, may hold values from 0 to 127, as said below
Outputs:
- attended: bfloat16 [2048, 768], P(('groups', 'seq'), 'head'), parts along dimension 0
- grad_query: bfloat16 [2048, 768], P(('groups', 'seq'), 'head'), parts along dimension 0
- grad_key: bfloat16 [2048, 768], P(('groups', 'seq'), 'head'), parts along dimension 0
- grad_value: bfloat16 [2048, 768], P(('groups', 'seq'), 'head'), parts along dimension 0
There are 2 independent parts, one for each index of `groups`. A program takes and returns all parts, laid end to end along the dimension named above; an argument that names none is the same for every part. Nothing has to cross between parts.
Inputs may be any that keep to these rules, and one draw needn't show every extreme that they name: offsets[l, h] lies in 0 to 2^l - 1 at level l, and at every level some head takes 2^l - 1.
All inputs are finite; a program needn't handle non-finite values.
Results may differ from a plain program's by a relative error of at most 0.019.
Values may be sent and summed in bfloat16 or wider, within the bound.
A program may use at most 128 MiB of HBM per device.

v0:
```python
import functools
import math

import jax
import jax.numpy as jnp
from jax import lax
from jax.experimental import pallas as pl
from jax.experimental.pallas import tpu as pltpu
from jax.sharding import PartitionSpec as P

HDIM = 48
LEVELS = 8


def swapped(shard, axis, bit):
    return lax.ppermute(shard, axis, [(i, i ^ 1 << bit) for i in range(lax.axis_size(axis))])


def pick_rows(values, level_offsets, stride):
    if stride == 1:
        return values
    length, head_count = (values.shape[0], values.shape[1])
    trailing = values.shape[2:]
    grouped = values.reshape((length // stride, stride, head_count) + trailing)
    marks = jnp.arange(stride, dtype=jnp.int32)[:, None] == level_offsets[None, :]
    marks = marks.reshape((1, stride, head_count) + (1,) * len(trailing))
    kept = jnp.where(marks, grouped, jnp.zeros((), values.dtype))
    return jnp.sum(kept, axis=1, dtype=values.dtype)


def spread_rows(values, level_offsets, stride, fill):
    count, head_count = (values.shape[0], values.shape[1])
    trailing = values.shape[2:]
    marks = jnp.arange(stride, dtype=jnp.int32)[:, None] == level_offsets[None, :]
    marks = marks.reshape((1, stride, head_count) + (1,) * len(trailing))
    placed = jnp.where(marks, values[:, None], jnp.asarray(fill, values.dtype))
    return placed.reshape((count * stride, head_count) + trailing)


def pair_bits(count):
    return list(range(count))


def send_pairs(block_rows, bit_no):
    return swapped(block_rows, "seq", bit_no)


def send_partials(block_rows, bit_no):
    return swapped(block_rows.astype(jnp.bfloat16), "seq", bit_no).astype(block_rows.dtype)


def double_up(block_rows, bit_list, sender):
    position = lax.axis_index("seq")
    for bit_no in bit_list:
        partner_rows = sender(block_rows, bit_no)
        upper_half = position // 2**bit_no % 2 == 1
        block_rows = jnp.where(
            upper_half,
            jnp.concatenate([partner_rows, block_rows], 0),
            jnp.concatenate([block_rows, partner_rows], 0),
        )
    return block_rows


def halve_down(buffer, bit_list, sender):
    position = lax.axis_index("seq")
    for bit_no in reversed(bit_list):
        half_rows = buffer.shape[0] // 2
        lower_part, upper_part = (buffer[:half_rows], buffer[half_rows:])
        upper_half = position // 2**bit_no % 2 == 1
        kept_half = jnp.where(upper_half, upper_part, lower_part)
        given_half = jnp.where(upper_half, lower_part, upper_part)
        buffer = kept_half + sender(given_half, bit_no)
    return buffer


def head_blocks(heads_here):
    block_width = min(heads_here, 4)
    return [
        (first, min(first + block_width, heads_here)) for first in range(0, heads_here, block_width)
    ]


def forward_level(query_seg, key_seg, value_seg, factor):
    largest_list, total_list, summed_list = ([], [], [])
    for first, last in head_blocks(query_seg.shape[2]):
        scores = (
            jnp.einsum(
                "nihd,njhd->nhij",
                query_seg[:, :, first:last],
                key_seg[:, :, first:last],
                preferred_element_type=jnp.float32,
            )
            * factor
        )
        largest = jnp.max(scores, axis=3)
        powers = jnp.exp(scores - largest[..., None])
        largest_list.append(largest)
        total_list.append(jnp.sum(powers, axis=3))
        summed_list.append(
            jnp.einsum(
                "nhij,njhd->nihd",
                powers.astype(jnp.bfloat16),
                value_seg[:, :, first:last],
                preferred_element_type=jnp.float32,
            )
        )
    return (
        jnp.concatenate(largest_list, 1),
        jnp.concatenate(total_list, 1),
        jnp.concatenate(summed_list, 2),
    )


def level_grads(query_seg, key_seg, value_seg, outgrad_seg, total_seg, dot_seg, factor):
    query_list, key_list, value_list = ([], [], [])
    for first, last in head_blocks(query_seg.shape[2]):
        query_part = query_seg[:, :, first:last]
        key_block = key_seg[:, :, first:last]
        outgrad_part = outgrad_seg[:, :, first:last]
        scores = (
            jnp.einsum("nihd,njhd->nhij", query_part, key_block, preferred_element_type=jnp.float32)
            * factor
        )
        weights = jnp.exp(scores - total_seg[:, first:last, :, None])
        grad_prob = jnp.einsum(
            "nihd,njhd->nhij",
            outgrad_part,
            value_seg[:, :, first:last],
            preferred_element_type=jnp.float32,
        )
        grad_score = (weights * (grad_prob - dot_seg[:, first:last, :, None])).astype(jnp.bfloat16)
        query_list.append(
            jnp.einsum("nhij,njhd->nihd", grad_score, key_block, preferred_element_type=jnp.float32)
            * factor
        )
        key_list.append(
            jnp.einsum(
                "nhij,nihd->njhd", grad_score, query_part, preferred_element_type=jnp.float32
            )
            * factor
        )
        value_list.append(
            jnp.einsum(
                "nhij,nihd->njhd",
                weights.astype(jnp.bfloat16),
                outgrad_part,
                preferred_element_type=jnp.float32,
            )
        )
    query_grad = jnp.concatenate(query_list, 2)
    key_grad = jnp.concatenate(key_list, 2)
    value_grad = jnp.concatenate(value_list, 2)
    return (query_grad, key_grad, value_grad)


def general_body(queries, key_rows, value_rows, grad_out, offsets):
    row_count = queries.shape[0]
    width_here = queries.shape[1]
    heads_here = width_here // HDIM
    factor = HDIM ** (-0.5)
    seq_count = lax.axis_size("seq")
    segment = row_count * seq_count // 2 ** (LEVELS - 1)
    head_first = lax.axis_index("head") * heads_here
    offsets_here = lax.dynamic_slice_in_dim(offsets, head_first, heads_here, 1)
    query_all = queries.reshape(row_count, heads_here, HDIM)
    key_all = key_rows.reshape(row_count, heads_here, HDIM)
    value_all = value_rows.reshape(row_count, heads_here, HDIM)
    outgrad_all = grad_out.reshape(row_count, heads_here, HDIM)
    levels_kept = []
    for level_no in range(LEVELS):
        stride = 2**level_no
        seg_span = segment * stride
        picked = row_count // stride
        level_offsets = offsets_here[level_no]
        query_lev = pick_rows(query_all, level_offsets, stride)
        key_lev = pick_rows(key_all, level_offsets, stride)
        value_lev = pick_rows(value_all, level_offsets, stride)
        if seg_span <= row_count:
            pieces = row_count // seg_span
            bit_list = []
            query_seg = query_lev.reshape(pieces, segment, heads_here, HDIM)
            key_seg = key_lev.reshape(pieces, segment, heads_here, HDIM)
            value_seg = value_lev.reshape(pieces, segment, heads_here, HDIM)
        else:
            group_size = seg_span // row_count
            packed = jnp.concatenate(
                [key_lev.reshape(picked, width_here), value_lev.reshape(picked, width_here)], 1
            )
            if group_size == seq_count:
                bit_list = list(range(group_size.bit_length() - 1))
                gathered = lax.all_gather(packed, "seq", axis=0, tiled=True)
            else:
                bit_list = pair_bits(group_size.bit_length() - 1)
                gathered = double_up(packed, bit_list, send_pairs)
            query_seg = query_lev.reshape(1, picked, heads_here, HDIM)
            key_seg = gathered[:, :width_here].reshape(1, segment, heads_here, HDIM)
            value_seg = gathered[:, width_here:].reshape(1, segment, heads_here, HDIM)
        largest, totals, summed = forward_level(query_seg, key_seg, value_seg, factor)
        level_max = spread_rows(
            jnp.transpose(largest, (0, 2, 1)).reshape(picked, heads_here),
            level_offsets,
            stride,
            -jnp.inf,
        )
        level_total = spread_rows(
            jnp.transpose(totals, (0, 2, 1)).reshape(picked, heads_here), level_offsets, stride, 0.0
        )
        level_sum = spread_rows(
            summed.reshape(picked, heads_here, HDIM), level_offsets, stride, 0.0
        )
        if level_no == 0:
            running_max, running_total, running_sum = (level_max, level_total, level_sum)
        else:
            newest_max = jnp.maximum(running_max, level_max)
            old_scale = jnp.exp(running_max - newest_max)
            new_scale = jnp.exp(level_max - newest_max)
            running_total = running_total * old_scale + level_total * new_scale
            running_sum = running_sum * old_scale[..., None] + level_sum * new_scale[..., None]
            running_max = newest_max
        levels_kept.append(
            (
                stride,
                level_offsets,
                seg_span,
                bit_list,
                query_lev,
                key_lev,
                value_lev,
                query_seg,
                key_seg,
                value_seg,
            )
        )
    attended = (running_sum / running_total[..., None]).astype(jnp.bfloat16)
    log_total = running_max + jnp.log(running_total)
    dot_rows = jnp.sum(outgrad_all.astype(jnp.float32) * attended.astype(jnp.float32), axis=2)
    grad_q_sum = jnp.zeros((row_count, heads_here, HDIM), jnp.float32)
    grad_k_sum = jnp.zeros((row_count, heads_here, HDIM), jnp.float32)
    grad_v_sum = jnp.zeros((row_count, heads_here, HDIM), jnp.float32)
    for (
        stride,
        level_offsets,
        seg_span,
        bit_list,
        query_lev,
        key_lev,
        value_lev,
        query_seg,
        key_seg,
        value_seg,
    ) in levels_kept:
        picked = row_count // stride
        outgrad_lev = pick_rows(outgrad_all, level_offsets, stride)
        total_lev = pick_rows(log_total, level_offsets, stride)
        dot_lev = pick_rows(dot_rows, level_offsets, stride)
        pieces = query_seg.shape[0]
        rows_each = query_seg.shape[1]
        outgrad_seg = outgrad_lev.reshape(pieces, rows_each, heads_here, HDIM)
        total_seg = jnp.transpose(total_lev.reshape(pieces, rows_each, heads_here), (0, 2, 1))
        dot_seg = jnp.transpose(dot_lev.reshape(pieces, rows_each, heads_here), (0, 2, 1))
        if seg_span <= row_count:
            grad_query_lev, key_part, value_part = level_grads(
                query_seg, key_seg, value_seg, outgrad_seg, total_seg, dot_seg, factor
            )
            key_grad = key_part.reshape(picked, heads_here, HDIM)
            value_grad = value_part.reshape(picked, heads_here, HDIM)
        else:
            grad_query_lev, key_part, value_part = level_grads(
                query_seg, key_seg, value_seg, outgrad_seg, total_seg, dot_seg, factor
            )
            packed = jnp.concatenate(
                [key_part.reshape(segment, width_here), value_part.reshape(segment, width_here)], 1
            )
            own_rows = halve_down(packed, bit_list, send_partials)
            key_grad = own_rows[:, :width_here].reshape(picked, heads_here, HDIM)
            value_grad = own_rows[:, width_here:].reshape(picked, heads_here, HDIM)
        grad_q_sum = grad_q_sum + spread_rows(
            grad_query_lev.reshape(picked, heads_here, HDIM), level_offsets, stride, 0.0
        )
        grad_k_sum = grad_k_sum + spread_rows(key_grad, level_offsets, stride, 0.0)
        grad_v_sum = grad_v_sum + spread_rows(value_grad, level_offsets, stride, 0.0)
    return (
        attended.reshape(row_count, width_here),
        grad_q_sum.reshape(row_count, width_here).astype(jnp.bfloat16),
        grad_k_sum.reshape(row_count, width_here).astype(jnp.bfloat16),
        grad_v_sum.reshape(row_count, width_here).astype(jnp.bfloat16),
    )


SEG = 8
LOCAL = 5
NEG = -1e30
NN = (((1,), (0,)), ((), ()))
NT = (((1,), (1,)), ((), ()))


def mm(lhs, rhs, dims=NN):
    return lax.dot_general(lhs, rhs, dims, preferred_element_type=jnp.float32)


def flipped(block):
    return block.astype(jnp.float32).T.astype(jnp.bfloat16)


def window(head_no):
    first = head_no * HDIM
    return first // 128 * 128, -(-(first + HDIM) // 128) * 128


def zero_extended(rows, head_no):
    low, high = window(head_no)
    first = head_no * HDIM
    parts = []
    if first > low:
        parts.append(jnp.zeros((first - low, rows.shape[1]), rows.dtype))
    parts.append(rows[first : first + HDIM])
    if high > first + HDIM:
        parts.append(jnp.zeros((high - first - HDIM, rows.shape[1]), rows.dtype))
    return parts[0] if len(parts) == 1 else jnp.concatenate(parts, 0)


def kernel(
    seq_count, heads, offs, q_ref, k_ref, v_ref, g_ref,
    att_ref, dq_ref, dk_ref, dv_ref,
    buf5, buf6, buf7, stat, build, slots, e_scr, dp_scr,
    send5, recv5, send6, recv6, send7, recv7, send_st, recv_st,
):
    me = lax.axis_index("seq")
    f32, bf16 = jnp.float32, jnp.bfloat16
    factor = HDIM ** (-0.5)
    factor2 = factor * math.log2(math.e)
    rows = q_ref.shape[0]
    width = q_ref.shape[1]
    head_first = lax.axis_index("head") * heads

    def peer(dist):
        low = lax.rem(me, 2)
        mid = lax.rem(me // 2, 2)
        top = me // 4
        b0, b1, b2 = dist & 1, dist >> 1 & 1, dist >> 2
        low = 1 - low if b0 else low
        mid = 1 - mid if b1 else mid
        top = 1 - top if b2 else top
        return top * 4 + mid * 2 + low

    barrier = pltpu.get_barrier_semaphore()
    for dist in range(1, seq_count):
        pl.semaphore_signal(
            barrier, inc=1, device_id={"seq": peer(dist)}, device_id_type=pl.DeviceIdType.MESH
        )

    off = [[offs[lev, head_first + h] for h in range(heads)] for lev in range(LEVELS)]
    refs = (q_ref, k_ref, v_ref, g_ref)

    slot_no = lax.broadcasted_iota(jnp.int32, (SEG, rows), 0)
    lane_no = lax.broadcasted_iota(jnp.int32, (SEG, rows), 1)
    picks = []
    for h in range(heads):
        target = jnp.where(
            slot_no < 4,
            slot_no * 32 + off[5][h],
            jnp.where(slot_no < 6, (slot_no - 4) * 64 + off[6][h], off[7][h]),
        )
        target = jnp.where(slot_no == 7, -1, target)
        picks.append(target == lane_no)
    chosen = jnp.concatenate([jnp.where(p, 1.0, 0.0) for p in picks], 0).astype(bf16)
    col_head = lax.broadcasted_iota(jnp.int32, (SEG, width), 1)
    for a in range(4):
        got = mm(chosen, refs[a][...])
        own = jnp.zeros((SEG, width), f32)
        for h in range(heads):
            inside = (col_head >= h * HDIM) & (col_head < (h + 1) * HDIM)
            own = jnp.where(inside, got[h * SEG : (h + 1) * SEG], own)
        build[4 * a : 4 * a + 4, :] = own[0:4]
        build[16 + 2 * a : 18 + 2 * a, :] = own[4:6]
        for c in range(3):
            build[32 + 4 * a + c : 33 + 4 * a + c, 0:128] = own[6:7, 128 * c : 128 * c + 128]
        build[35 + 4 * a : 36 + 4 * a, 0:128] = jnp.zeros((1, 128), f32)
    build[24:32, :] = jnp.zeros((8, width), f32)
    buf5[0] = build[0:16, :].astype(bf16)
    buf6[0] = build[16:32, :].astype(bf16)
    buf7[0] = build[32:48, 0:128].astype(bf16)

    pl.semaphore_wait(barrier, seq_count - 1)

    def remote(buf, send, recv, dist):
        return pltpu.make_async_remote_copy(
            src_ref=buf.at[0],
            dst_ref=buf.at[dist],
            send_sem=send.at[dist],
            recv_sem=recv.at[dist],
            device_id={"seq": peer(dist)},
            device_id_type=pl.DeviceIdType.MESH,
        )

    first = [remote(buf7, send7, recv7, d) for d in (7, 6, 5, 4, 3, 2, 1)]
    first += [remote(buf6, send6, recv6, d) for d in (3, 2, 1)]
    first += [remote(buf5, send5, recv5, 1)]
    for copy in first:
        copy.start()

    qt, kt, vt, gt = [flipped(r[...]) for r in refs]

    feat_no = lax.broadcasted_iota(jnp.int32, (32, rows), 0)
    pos = lax.broadcasted_iota(jnp.int32, (32, rows), 1)
    feats = []
    starts = (0, 16, 24, 28, 30)
    place = feat_no - 0
    seg_of = pos // 8
    rest = pos & 0
    for lev in range(1, LOCAL):
        past = feat_no >= starts[lev]
        place = jnp.where(past, feat_no - starts[lev], place)
        seg_of = jnp.where(past, pos // (8 << lev), seg_of)
        rest = jnp.where(past, pos & ((1 << lev) - 1), rest)
    in_seg = (place == seg_of) & (feat_no < 31)
    for h in range(heads):
        wanted = jnp.where(feat_no >= 16, off[1][h], 0)
        for lev in range(2, LOCAL):
            wanted = jnp.where(feat_no >= starts[lev], off[lev][h], wanted)
        feats.append(jnp.where(in_seg & (rest == wanted), 1.0, 0.0))
    feat_rows = [
        jnp.concatenate(feats[4 * b : 4 * b + 4], 0).T.astype(bf16) for b in range(heads // 4)
    ]
    tops = []
    counts = []
    for h in range(heads):
        low, high = window(h)
        before = 32 * (h % 4)
        parts = [jnp.zeros((before, rows), bf16)] if before else []
        parts.append(feats[h].astype(bf16))
        if before < 96:
            parts.append(jnp.zeros((96 - before, rows), bf16))
        count = mm(feat_rows[h // 4], jnp.concatenate(parts, 0))
        score = mm(k_ref[:, low:high], zero_extended(qt, h)) * factor2
        score = jnp.where(count > 0, score, NEG)
        top = jnp.max(score, axis=0, keepdims=True)
        tops.append(top)
        e_scr[h] = count * jnp.exp2(score - top)
        dp_scr[h] = mm(v_ref[:, low:high], zero_extended(gt, h))

    for copy in first:
        copy.wait()
    kinds = []
    for a in range(4):
        for d in range(2):
            slots[4 * d : 4 * d + 4, :] = buf5[d].astype(f32)[4 * a : 4 * a + 4]
        for d in range(4):
            slots[8 + 2 * d : 10 + 2 * d, :] = buf6[d].astype(f32)[2 * a : 2 * a + 2]
        for d in range(8):
            for c in range(3):
                slots[16 + d : 17 + d, 128 * c : 128 * c + 128] = buf7[d].astype(f32)[
                    4 * a + c : 4 * a + c + 1
                ]
        slots[24:32, :] = jnp.zeros((8, width), f32)
        kinds.append(slots[...])
    q_sl, k_sl, v_sl, g_sl = [x.astype(bf16) for x in kinds]
    q_st, k_st, v_st, g_st = [x.T.astype(bf16) for x in kinds]

    row32 = lax.broadcasted_iota(jnp.int32, (32, rows), 0)
    lane32 = lax.broadcasted_iota(jnp.int32, (32, rows), 1)
    span = jnp.where(row32 < 8, 31, jnp.where(row32 < 16, 63, 127))
    rest32 = lane32 & span
    held = []
    parts_far = []
    delta_rows = []
    inv_rows = []
    note = jnp.zeros((SEG, 128), f32)
    lane8 = lax.broadcasted_iota(jnp.int32, (SEG, 128), 1)
    for h in range(heads):
        low, high = window(h)
        cut = slice(h * HDIM, (h + 1) * HDIM)
        wanted = jnp.where(row32 < 8, off[5][h], jnp.where(row32 < 16, off[6][h], off[7][h]))
        inside = (rest32 == wanted) & (row32 < 24)
        held.append(inside)
        far = mm(k_sl[:, low:high], zero_extended(qt, h)) * factor2
        far = jnp.where(inside, far, NEG)
        top = jnp.maximum(tops[h], jnp.max(far, axis=0, keepdims=True))
        e_far = jnp.exp2(far - top)
        shrink = jnp.exp2(tops[h] - top)
        near = e_scr[h]
        total = jnp.sum(near, axis=0, keepdims=True) * shrink + jnp.sum(
            e_far, axis=0, keepdims=True
        )
        inv = 1.0 / total
        near = near * (shrink * inv)
        e_far = e_far * inv
        e_scr[h] = near
        out = mm(vt[cut], near.astype(bf16)) + mm(v_st[cut], e_far.astype(bf16))
        out = out.astype(bf16).astype(f32)
        att_ref[cut, :] = out
        delta = jnp.sum(out * gt[cut].astype(f32), axis=0, keepdims=True)
        delta_rows.append(delta)
        parts_far.append(e_far)
        lse = top + jnp.log2(total)
        lse_col = jnp.sum(jnp.where(picks[h], lse, 0.0), axis=1, keepdims=True)
        delta_col = jnp.sum(jnp.where(picks[h], delta, 0.0), axis=1, keepdims=True)
        note = jnp.where(lane8 == h, lse_col, note)
        note = jnp.where(lane8 == heads + h, delta_col, note)
    stat[0] = note
    second = [remote(stat, send_st, recv_st, d) for d in (7, 6, 5, 4, 3, 2, 1)]
    for copy in second:
        copy.start()

    near_k, near_v, far_s, far_p = [], [], [], []
    for h in range(heads):
        low, high = window(h)
        cut = slice(h * HDIM, (h + 1) * HDIM)
        near = e_scr[h]
        ds = (near * (dp_scr[h] - delta_rows[h])).astype(bf16)
        dp_far = mm(v_sl[:, low:high], zero_extended(gt, h))
        ds_far = (parts_far[h] * (dp_far - delta_rows[h])).astype(bf16)
        dq_ref[cut, :] = (mm(kt[cut], ds) + mm(k_st[cut], ds_far)) * factor
        dk_ref[cut, :] = mm(qt[cut], ds, NT)
        dv_ref[cut, :] = mm(gt[cut], near.astype(bf16), NT)
        far_s.append(mm(q_sl[:, low:high], zero_extended(kt, h)) * factor2)
        far_p.append(mm(g_sl[:, low:high], zero_extended(vt, h)))

    for copy in second:
        copy.wait()
    for d in range(2):
        slots[4 * d : 4 * d + 4, 0:128] = stat[d, 0:4]
    for d in range(4):
        slots[8 + 2 * d : 10 + 2 * d, 0:128] = stat[d, 4:6]
    for d in range(8):
        slots[16 + d : 17 + d, 0:128] = stat[d, 6:7]
    notes = slots[:, 0:128]
    for h in range(heads):
        cut = slice(h * HDIM, (h + 1) * HDIM)
        lse = notes[:, h : h + 1]
        delta = notes[:, heads + h : heads + h + 1]
        prob = jnp.exp2(jnp.where(held[h], far_s[h] - lse, NEG))
        ds = (prob * (far_p[h] - delta)).astype(bf16)
        dk_ref[cut, :] = (dk_ref[cut, :] + mm(q_st[cut], ds)) * factor
        dv_ref[cut, :] = dv_ref[cut, :] + mm(g_st[cut], prob.astype(bf16))


def small_body(queries, key_rows, value_rows, grad_out, offsets):
    rows, width = queries.shape
    heads = width // HDIM
    seq_count = lax.axis_size("seq")
    vmem = pl.BlockSpec(memory_space=pltpu.VMEM)
    dma = pltpu.SemaphoreType.DMA
    outs = pl.pallas_call(
        functools.partial(kernel, seq_count, heads),
        out_shape=[jax.ShapeDtypeStruct((width, rows), jnp.float32)] * 4,
        in_specs=[pl.BlockSpec(memory_space=pltpu.SMEM)] + [vmem] * 4,
        out_specs=[vmem] * 4,
        scratch_shapes=[
            pltpu.VMEM((2, 16, width), jnp.bfloat16),
            pltpu.VMEM((4, 16, width), jnp.bfloat16),
            pltpu.VMEM((8, 16, 128), jnp.bfloat16),
            pltpu.VMEM((8, SEG, 128), jnp.float32),
            pltpu.VMEM((48, width), jnp.float32),
            pltpu.VMEM((32, width), jnp.float32),
            pltpu.VMEM((heads, rows, rows), jnp.float32),
            pltpu.VMEM((heads, rows, rows), jnp.float32),
            dma((2,)), dma((2,)), dma((4,)), dma((4,)),
            dma((8,)), dma((8,)), dma((8,)), dma((8,)),
        ],
        compiler_params=pltpu.CompilerParams(
            collective_id=0, has_side_effects=True, vmem_limit_bytes=32 * 2**20
        ),
    )(offsets, queries, key_rows, value_rows, grad_out)
    return tuple(x.T.astype(jnp.bfloat16) for x in outs)


def body(queries, key_rows, value_rows, grad_out, offsets):
    rows, width = queries.shape
    seq_count = lax.axis_size("seq")
    if seq_count == 8 and rows == 128 and width == 8 * HDIM:
        return small_body(queries, key_rows, value_rows, grad_out, offsets)
    return general_body(queries, key_rows, value_rows, grad_out, offsets)


def solution(mesh):
    placed = (
        P(("groups", "seq"), "head"),
        P(("groups", "seq"), "head"),
        P(("groups", "seq"), "head"),
        P(("groups", "seq"), "head"),
        P(),
    )
    return jax.shard_map(
        body,
        mesh=mesh,
        in_specs=placed,
        out_specs=(
            P(("groups", "seq"), "head"),
            P(("groups", "seq"), "head"),
            P(("groups", "seq"), "head"),
            P(("groups", "seq"), "head"),
        ),
        check_vma=False,
    )
```

profile of v0, /device:TPU:0, one launch (start us, length us, event | category | flops | bytes accessed | tf_op | source)
XLA Modules:
  0.0 24.4 jit_solution(18006393608018818213)
XLA Ops:
  0.6 0.0 copy-start
  0.6 0.9 %copy-done = bf16[128,384]{1,0:T(8,128)(2,1)S(1)} copy-done((bf16[128,384]{1,0:T(8,128)(2,1)S(1)}, bf16[128,384]{1,0:T(8,128)(2,1)}, u32[]{:S(2)}) %copy-start) | copy-done | bytes 98328
  1.5 0.0 copy-start.1
  1.5 0.9 %copy-done.1 = bf16[128,384]{1,0:T(8,128)(2,1)S(1)} copy-done((bf16[128,384]{1,0:T(8,128)(2,1)S(1)}, bf16[128,384]{1,0:T(8,128)(2,1)}, u32[]{:S(2)}) %copy-start.1) | copy-done | bytes 98328
  2.4 0.0 copy-start.2
  2.4 0.9 %copy-done.2 = bf16[128,384]{1,0:T(8,128)(2,1)S(1)} copy-done((bf16[128,384]{1,0:T(8,128)(2,1)S(1)}, bf16[128,384]{1,0:T(8,128)(2,1)}, u32[]{:S(2)}) %copy-start.2) | copy-done | bytes 98328
  3.3 0.0 copy-start.3
  3.3 0.9 %copy-done.3 = bf16[128,384]{1,0:T(8,128)(2,1)S(1)} copy-done((bf16[128,384]{1,0:T(8,128)(2,1)S(1)}, bf16[128,384]{1,0:T(8,128)(2,1)}, u32[]{:S(2)}) %copy-start.3) | copy-done | bytes 98328
  4.2 0.0 copy-start.4
  4.2 0.7 %copy-done.4 = s32[8,16]{1,0:T(8,128)S(1)} copy-done((s32[8,16]{1,0:T(8,128)S(1)}, s32[8,16]{1,0:T(8,128)}, u32[]{:S(2)}) %copy-start.4) | copy-done | bytes 536
  4.9 16.4 %shard_map.84 = (f32[384,128]{1,0:T(8,128)S(1)}, f32[384,128]{1,0:T(8,128)S(1)}, f32[384,128]{1,0:T(8,128)S(1)}, f32[384,128]{1,0:T(8,128)S(1)}) custom-call(s32[8,16]{1,0:T(8,128)S(1)} %copy-done.4, bf16[128,384]{1,0:T(8,128)(2,1)S(1)} %copy-done, bf16[128,384]{1,0:T(8,128)(2,1)S(1)} %copy-done.1, bf16[128,384]{1,0:T(8,128)(2,1)S(1)} %copy-done.2, ...), custom_call_target="tpu_custom_call" | custom-call | tf_op jit(solution)/shard_map/pallas_call | solution.py:545
  21.3 0.8 %copy.10 = bf16[128,384]{1,0:T(8,128)(2,1)} copy(bf16[128,384]{0,1:T(8,128)(2,1)S(1)} %get-tuple-element.18) | data formatting | bytes 196608
  22.1 0.8 %copy.9 = bf16[128,384]{1,0:T(8,128)(2,1)} copy(bf16[128,384]{0,1:T(8,128)(2,1)S(1)} %get-tuple-element.19) | data formatting | bytes 196608
  22.9 0.8 %copy.12 = bf16[128,384]{1,0:T(8,128)(2,1)} copy(bf16[128,384]{0,1:T(8,128)(2,1)S(1)} %get-tuple-element.16) | data formatting | bytes 196608
  23.6 0.8 %copy.11 = bf16[128,384]{1,0:T(8,128)(2,1)} copy(bf16[128,384]{0,1:T(8,128)(2,1)S(1)} %get-tuple-element.17) | data formatting | bytes 196608
  (2 shorter events, 0.1 us)
Async XLA Ops:
  0.6 0.9 %copy-start = (bf16[128,384]{1,0:T(8,128)(2,1)S(1)}, bf16[128,384]{1,0:T(8,128)(2,1)}, u32[]{:S(2)}) copy-start(bf16[128,384]{1,0:T(8,128)(2,1)} %q_ref.1) | copy-start | bytes 294916
  1.5 0.9 %copy-start.1 = (bf16[128,384]{1,0:T(8,128)(2,1)S(1)}, bf16[128,384]{1,0:T(8,128)(2,1)}, u32[]{:S(2)}) copy-start(bf16[128,384]{1,0:T(8,128)(2,1)} %k_ref.1) | copy-start | bytes 294916
  2.4 0.9 %copy-start.2 = (bf16[128,384]{1,0:T(8,128)(2,1)S(1)}, bf16[128,384]{1,0:T(8,128)(2,1)}, u32[]{:S(2)}) copy-start(bf16[128,384]{1,0:T(8,128)(2,1)} %v_ref.1) | copy-start | bytes 294916
  3.3 0.9 %copy-start.3 = (bf16[128,384]{1,0:T(8,128)(2,1)S(1)}, bf16[128,384]{1,0:T(8,128)(2,1)}, u32[]{:S(2)}) copy-start(bf16[128,384]{1,0:T(8,128)(2,1)} %g_ref.1) | copy-start | bytes 294916
  4.2 0.7 %copy-start.4 = (s32[8,16]{1,0:T(8,128)S(1)}, s32[8,16]{1,0:T(8,128)}, u32[]{:S(2)}) copy-start(s32[8,16]{1,0:T(8,128)} %offs.1) | copy-start | bytes 1540
where the time goes:
time: 24.6 us; the launch traced here: 24.4 us
  Pallas kernels  16.4 us (67%)
  local copies, waits for them, and re-layouts  7.25 us (29%)
  between operations  0.67 us (3%)
    pallas_call x1, Pallas kernels, small_body(): pl.pallas_call(functools.partial(kernel, seq_count, heads), out_shape=[ja...  16.4 us
    unnamed x14, local copies, waits for them, and re-layouts  7.25 us

commit v1 on v0

--- a/solution.py
+++ b/solution.py
@@ -300,7 +300,7 @@
 
 
 def flipped(block):
-    return block.astype(jnp.float32).T.astype(jnp.bfloat16)
+    return block.astype(jnp.bfloat16).T
 
 
 def window(head_no):
@@ -321,12 +321,21 @@
 
 
 def kernel(
-    seq_count, heads, offs, q_ref, k_ref, v_ref, g_ref,
-    att_ref, dq_ref, dk_ref, dv_ref,
+    seq_count, heads, offs_hbm, q_hbm, k_hbm, v_hbm, g_hbm,
+    att_out, dq_out, dk_out, dv_out,
+    offs, q_ref, k_ref, v_ref, g_ref, att_ref, dq_ref, dk_ref, dv_ref, fetch,
     buf5, buf6, buf7, stat, build, slots, e_scr, dp_scr,
     send5, recv5, send6, recv6, send7, recv7, send_st, recv_st,
 ):
     me = lax.axis_index("seq")
+    fetches = [
+        pltpu.make_async_copy(here, there, fetch.at[i])
+        for i, (here, there) in enumerate(
+            ((offs_hbm, offs), (q_hbm, q_ref), (k_hbm, k_ref), (v_hbm, v_ref), (g_hbm, g_ref))
+        )
+    ]
+    for copy in fetches:
+        copy.start()
     f32, bf16 = jnp.float32, jnp.bfloat16
     factor = HDIM ** (-0.5)
     factor2 = factor * math.log2(math.e)
@@ -350,6 +359,8 @@
             barrier, inc=1, device_id={"seq": peer(dist)}, device_id_type=pl.DeviceIdType.MESH
         )
 
+    for copy in fetches:
+        copy.wait()
     off = [[offs[lev, head_first + h] for h in range(heads)] for lev in range(LEVELS)]
     refs = (q_ref, k_ref, v_ref, g_ref)
 
@@ -517,6 +528,8 @@
         far_s.append(mm(q_sl[:, low:high], zero_extended(kt, h)) * factor2)
         far_p.append(mm(g_sl[:, low:high], zero_extended(vt, h)))
 
+    att_out[...] = flipped(att_ref[...])
+    dq_out[...] = flipped(dq_ref[...])
     for copy in second:
         copy.wait()
     for d in range(2):
@@ -534,20 +547,36 @@
         ds = (prob * (far_p[h] - delta)).astype(bf16)
         dk_ref[cut, :] = (dk_ref[cut, :] + mm(q_st[cut], ds)) * factor
         dv_ref[cut, :] = dv_ref[cut, :] + mm(g_st[cut], prob.astype(bf16))
+    dk_out[...] = flipped(dk_ref[...])
+    dv_out[...] = flipped(dv_ref[...])
+
+
+def write_out(*refs):
+    ends = refs[8]
+    copies = [pltpu.make_async_copy(refs[i], refs[4 + i], ends.at[i]) for i in range(4)]
+    for copy in copies:
+        copy.start()
+    for copy in copies:
+        copy.wait()
 
 
 def small_body(queries, key_rows, value_rows, grad_out, offsets):
     rows, width = queries.shape
     heads = width // HDIM
     seq_count = lax.axis_size("seq")
+    hbm = pl.BlockSpec(memory_space=pltpu.HBM)
     vmem = pl.BlockSpec(memory_space=pltpu.VMEM)
     dma = pltpu.SemaphoreType.DMA
     outs = pl.pallas_call(
         functools.partial(kernel, seq_count, heads),
-        out_shape=[jax.ShapeDtypeStruct((width, rows), jnp.float32)] * 4,
-        in_specs=[pl.BlockSpec(memory_space=pltpu.SMEM)] + [vmem] * 4,
+        out_shape=[jax.ShapeDtypeStruct((rows, width), jnp.bfloat16)] * 4,
+        in_specs=[hbm] * 5,
         out_specs=[vmem] * 4,
         scratch_shapes=[
+            pltpu.SMEM(offsets.shape, jnp.int32),
+            *[pltpu.VMEM((rows, width), jnp.bfloat16)] * 4,
+            *[pltpu.VMEM((width, rows), jnp.float32)] * 4,
+            dma((5,)),
             pltpu.VMEM((2, 16, width), jnp.bfloat16),
             pltpu.VMEM((4, 16, width), jnp.bfloat16),
             pltpu.VMEM((8, 16, 128), jnp.bfloat16),
@@ -560,10 +589,16 @@
             dma((8,)), dma((8,)), dma((8,)), dma((8,)),
         ],
         compiler_params=pltpu.CompilerParams(
-            collective_id=0, has_side_effects=True, vmem_limit_bytes=32 * 2**20
+            collective_id=0, has_side_effects=True, vmem_limit_bytes=62 * 2**20
         ),
     )(offsets, queries, key_rows, value_rows, grad_out)
-    return tuple(x.T.astype(jnp.bfloat16) for x in outs)
+    return pl.pallas_call(
+        write_out,
+        out_shape=[jax.ShapeDtypeStruct((rows, width), jnp.bfloat16)] * 4,
+        in_specs=[vmem] * 4,
+        out_specs=[hbm] * 4,
+        scratch_shapes=[dma((4,))],
+    )(*outs)
 
 
 def body(queries, key_rows, value_rows, grad_out, offsets):

time: 24.6 us -> 20.2 us (0.82)
  local copies, waits for them, and re-layouts: 7.25 us -> 0 us
  Pallas kernels: 16.4 us -> 19.4 us
    unnamed x14 -> x0, local copies, waits for them, and re-layouts: 7.25 us -> none
    pallas_call x0 -> x1, Pallas kernels: none -> 1.81 us  [small_body(): pl.pallas_call(write_out, out_shape=[jax.ShapeDtypeStruct((rows, width),...]
    pallas_call x1, Pallas kernels: 16.4 us -> 17.6 us  [small_body(): pl.pallas_call(functools.partial(kernel, seq_count, heads), out_shape=[ja...]
where the time goes in v1:
time: 20.2 us; the launch traced here: 20 us
  Pallas kernels  19.4 us (96%)
  between operations  0.64 us (3%)
    pallas_call x1, Pallas kernels, small_body(): pl.pallas_call(functools.partial(kernel, seq_count, heads), out_shape=[ja...  17.6 us
    pallas_call x1, Pallas kernels, small_body(): pl.pallas_call(write_out, out_shape=[jax.ShapeDtypeStruct((rows, width),...  1.81 us

profile of v1, /device:TPU:0, one launch (start us, length us, event | category | flops | bytes accessed | tf_op | source)
XLA Modules:
  0.0 20.0 jit_solution(14018632277488326453)
XLA Ops:
  0.6 17.6 %shard_map.84 = (bf16[128,384]{1,0:T(8,128)(2,1)}, bf16[128,384]{1,0:T(8,128)(2,1)}, bf16[128,384]{1,0:T(8,128)(2,1)}, bf16[128,384]{1,0:T(8,128)(2,1)}) custom-call(s32[8,16]{1,0:T(8,128)} %offs_hbm.1, bf16[128,384]{1,0:T(8,128)(2,1)} %q_hbm.1, bf16[128,384]{1,0:T(8,128)(2,1)} %k_hbm.1, bf16[128,384]{1,0:T(8,128)(2,1)} %v_hbm.1, bf16[128,384]{1,0:T(8,128)(2,1)} %g_hbm.1), custom_call_target="tpu_custom_call" | custom-call | tf_op jit(solution)/shard_map/pallas_call | solution.py:570
  18.2 1.8 %shard_map.85 = (bf16[128,384]{1,0:T(8,128)(2,1)}, bf16[128,384]{1,0:T(8,128)(2,1)}, bf16[128,384]{1,0:T(8,128)(2,1)}, bf16[128,384]{1,0:T(8,128)(2,1)}) custom-call(bf16[128,384]{1,0:T(8,128)(2,1)} %get-tuple-element.8.refs_0_, bf16[128,384]{1,0:T(8,128)(2,1)} %get-tuple-element.9.refs_1_, bf16[128,384]{1,0:T(8,128)(2,1)} %get-tuple-element.10.refs_2_, ...), custom_call_target="tpu_custom_call" | custom-call | tf_op jit(solution)/shard_map/pallas_call | solution.py:595

commit v2 on v1

--- a/solution.py
+++ b/solution.py
@@ -324,8 +324,8 @@
     seq_count, heads, offs_hbm, q_hbm, k_hbm, v_hbm, g_hbm,
     att_out, dq_out, dk_out, dv_out,
     offs, q_ref, k_ref, v_ref, g_ref, att_ref, dq_ref, dk_ref, dv_ref, fetch,
-    buf5, buf6, buf7, stat, build, slots, e_scr, dp_scr,
-    send5, recv5, send6, recv6, send7, recv7, send_st, recv_st,
+    buf_kv, buf_qg, stat, e_scr, dp_scr,
+    send_kv, recv_kv, send_qg, recv_qg, send_st, recv_st,
 ):
     me = lax.axis_index("seq")
     fetches = [
@@ -377,21 +377,20 @@
         picks.append(target == lane_no)
     chosen = jnp.concatenate([jnp.where(p, 1.0, 0.0) for p in picks], 0).astype(bf16)
     col_head = lax.broadcasted_iota(jnp.int32, (SEG, width), 1)
+    owns = []
     for a in range(4):
         got = mm(chosen, refs[a][...])
         own = jnp.zeros((SEG, width), f32)
         for h in range(heads):
             inside = (col_head >= h * HDIM) & (col_head < (h + 1) * HDIM)
             own = jnp.where(inside, got[h * SEG : (h + 1) * SEG], own)
-        build[4 * a : 4 * a + 4, :] = own[0:4]
-        build[16 + 2 * a : 18 + 2 * a, :] = own[4:6]
-        for c in range(3):
-            build[32 + 4 * a + c : 33 + 4 * a + c, 0:128] = own[6:7, 128 * c : 128 * c + 128]
-        build[35 + 4 * a : 36 + 4 * a, 0:128] = jnp.zeros((1, 128), f32)
-    build[24:32, :] = jnp.zeros((8, width), f32)
-    buf5[0] = build[0:16, :].astype(bf16)
-    buf6[0] = build[16:32, :].astype(bf16)
-    buf7[0] = build[32:48, 0:128].astype(bf16)
+        owns.append(own)
+    q_own, k_own, v_own, g_own = owns
+    last_row = lax.broadcasted_iota(jnp.int32, (SEG, width), 0) == SEG - 1
+    k_own = jnp.where(last_row, q_own[6:7], k_own)
+    v_own = jnp.where(last_row, g_own[6:7], v_own)
+    buf_kv[0] = jnp.concatenate([k_own, v_own], 0).astype(bf16)
+    buf_qg[0] = jnp.concatenate([q_own, g_own], 0).astype(bf16)
 
     pl.semaphore_wait(barrier, seq_count - 1)
 
@@ -405,9 +404,8 @@
             device_id_type=pl.DeviceIdType.MESH,
         )
 
-    first = [remote(buf7, send7, recv7, d) for d in (7, 6, 5, 4, 3, 2, 1)]
-    first += [remote(buf6, send6, recv6, d) for d in (3, 2, 1)]
-    first += [remote(buf5, send5, recv5, 1)]
+    first = [remote(buf_kv, send_kv, recv_kv, d) for d in (7, 6, 5, 4, 3, 2, 1)]
+    first += [remote(buf_qg, send_qg, recv_qg, d) for d in (3, 2, 1)]
     for copy in first:
         copy.start()
 
@@ -434,8 +432,10 @@
     feat_rows = [
         jnp.concatenate(feats[4 * b : 4 * b + 4], 0).T.astype(bf16) for b in range(heads // 4)
     ]
-    tops = []
-    counts = []
+    tops, sums, dots = [], [], []
+    lane8 = lax.broadcasted_iota(jnp.int32, (SEG, 128), 1)
+    row8 = lax.broadcasted_iota(jnp.int32, (SEG, 128), 0)
+    note = jnp.where((row8 == SEG - 1) & (lane8 >= heads) & (lane8 < 2 * heads), 1.0, 0.0)
     for h in range(heads):
         low, high = window(h)
         before = 32 * (h % 4)
@@ -447,106 +447,124 @@
         score = mm(k_ref[:, low:high], zero_extended(qt, h)) * factor2
         score = jnp.where(count > 0, score, NEG)
         top = jnp.max(score, axis=0, keepdims=True)
+        near = count * jnp.exp2(score - top)
+        dp = mm(v_ref[:, low:high], zero_extended(gt, h))
+        e_scr[h] = near
+        dp_scr[h] = dp
+        total = jnp.sum(near, axis=0, keepdims=True)
+        dot = jnp.sum(near * dp, axis=0, keepdims=True)
         tops.append(top)
-        e_scr[h] = count * jnp.exp2(score - top)
-        dp_scr[h] = mm(v_ref[:, low:high], zero_extended(gt, h))
-
-    for copy in first:
-        copy.wait()
-    kinds = []
-    for a in range(4):
-        for d in range(2):
-            slots[4 * d : 4 * d + 4, :] = buf5[d].astype(f32)[4 * a : 4 * a + 4]
-        for d in range(4):
-            slots[8 + 2 * d : 10 + 2 * d, :] = buf6[d].astype(f32)[2 * a : 2 * a + 2]
-        for d in range(8):
-            for c in range(3):
-                slots[16 + d : 17 + d, 128 * c : 128 * c + 128] = buf7[d].astype(f32)[
-                    4 * a + c : 4 * a + c + 1
-                ]
-        slots[24:32, :] = jnp.zeros((8, width), f32)
-        kinds.append(slots[...])
-    q_sl, k_sl, v_sl, g_sl = [x.astype(bf16) for x in kinds]
-    q_st, k_st, v_st, g_st = [x.T.astype(bf16) for x in kinds]
-
-    row32 = lax.broadcasted_iota(jnp.int32, (32, rows), 0)
-    lane32 = lax.broadcasted_iota(jnp.int32, (32, rows), 1)
-    span = jnp.where(row32 < 8, 31, jnp.where(row32 < 16, 63, 127))
-    rest32 = lane32 & span
-    held = []
-    parts_far = []
-    delta_rows = []
-    inv_rows = []
-    note = jnp.zeros((SEG, 128), f32)
-    lane8 = lax.broadcasted_iota(jnp.int32, (SEG, 128), 1)
-    for h in range(heads):
-        low, high = window(h)
-        cut = slice(h * HDIM, (h + 1) * HDIM)
-        wanted = jnp.where(row32 < 8, off[5][h], jnp.where(row32 < 16, off[6][h], off[7][h]))
-        inside = (rest32 == wanted) & (row32 < 24)
-        held.append(inside)
-        far = mm(k_sl[:, low:high], zero_extended(qt, h)) * factor2
-        far = jnp.where(inside, far, NEG)
-        top = jnp.maximum(tops[h], jnp.max(far, axis=0, keepdims=True))
-        e_far = jnp.exp2(far - top)
-        shrink = jnp.exp2(tops[h] - top)
-        near = e_scr[h]
-        total = jnp.sum(near, axis=0, keepdims=True) * shrink + jnp.sum(
-            e_far, axis=0, keepdims=True
-        )
-        inv = 1.0 / total
-        near = near * (shrink * inv)
-        e_far = e_far * inv
-        e_scr[h] = near
-        out = mm(vt[cut], near.astype(bf16)) + mm(v_st[cut], e_far.astype(bf16))
-        out = out.astype(bf16).astype(f32)
-        att_ref[cut, :] = out
-        delta = jnp.sum(out * gt[cut].astype(f32), axis=0, keepdims=True)
-        delta_rows.append(delta)
-        parts_far.append(e_far)
-        lse = top + jnp.log2(total)
-        lse_col = jnp.sum(jnp.where(picks[h], lse, 0.0), axis=1, keepdims=True)
-        delta_col = jnp.sum(jnp.where(picks[h], delta, 0.0), axis=1, keepdims=True)
-        note = jnp.where(lane8 == h, lse_col, note)
-        note = jnp.where(lane8 == heads + h, delta_col, note)
+        sums.append(total)
+        dots.append(dot)
+        for kind, row in enumerate((top, total, dot)):
+            column = jnp.sum(jnp.where(picks[h], row, 0.0), axis=1, keepdims=True)
+            here = (lane8 == kind * heads + h) & (row8 < SEG - 1)
+            note = jnp.where(here, column, note)
     stat[0] = note
     second = [remote(stat, send_st, recv_st, d) for d in (7, 6, 5, 4, 3, 2, 1)]
     for copy in second:
         copy.start()
 
-    near_k, near_v, far_s, far_p = [], [], [], []
+    far_n = SEG * seq_count
+    query_n = 5 * SEG
+    key_no = lax.broadcasted_iota(jnp.int32, (far_n, 128), 0)
+    key_slot = key_no & 7
+    key_dist = key_no >> 3
+    lane_pos = lax.broadcasted_iota(jnp.int32, (far_n, 128), 1)
+    key_span = jnp.where(key_slot < 4, 31, jnp.where(key_slot < 6, 63, 127))
+    key_reach = jnp.where(key_slot < 4, 1, jnp.where(key_slot < 6, 2, 3))
+    lane_rest = lane_pos & key_span
+    lane_ok = (key_dist >> key_reach) == 0
+
+    def query_marks(shape):
+        number = lax.broadcasted_iota(jnp.int32, shape, 1)
+        dist = jnp.where(number < 32, number >> 3, number - 32)
+        slot = jnp.where(number < 32, number & 7, 6)
+        return number, dist, slot
+
+    _, dist_b, slot_b = query_marks((far_n, query_n))
+    pair_ok = ((dist_b ^ key_dist[:, :query_n]) >> key_reach[:, :query_n]) == 0
+    number_c, dist_c, slot_c = query_marks((rows, query_n))
+    reach_c = jnp.where(slot_c < 4, 1, jnp.where(slot_c < 6, 2, 3))
+    span_c = jnp.where(slot_c < 4, 31, jnp.where(slot_c < 6, 63, 127))
+    own_pos = lax.broadcasted_iota(jnp.int32, (rows, query_n), 0)
+    rest_c = own_pos & span_c
+    ok_c = ((dist_c >> reach_c) == 0) & (slot_c != 7) & ((number_c < 32) | (dist_c >= 4))
+
+    for copy in first:
+        copy.wait()
+    kv = buf_kv[...].astype(f32)
+    qg = buf_qg[...].astype(f32)
+    k_far32 = kv[:, 0:SEG].reshape(far_n, width)
+    v_far32 = kv[:, SEG:].reshape(far_n, width)
+    q_far32 = jnp.concatenate(
+        [qg[:, 0:SEG].reshape(4 * SEG, width)] + [kv[d, SEG - 1 : SEG] for d in range(8)], 0
+    )
+    g_far32 = jnp.concatenate(
+        [qg[:, SEG:].reshape(4 * SEG, width)] + [kv[d, 2 * SEG - 1 : 2 * SEG] for d in range(8)], 0
+    )
+    k_far, v_far = k_far32.astype(bf16), v_far32.astype(bf16)
+    k_ft, v_ft, q_ft, g_ft = [
+        x.T.astype(bf16) for x in (k_far32, v_far32, q_far32, g_far32)
+    ]
+    for copy in second:
+        copy.wait()
+    st = stat[...]
+    notes = jnp.concatenate(
+        [st[0:4].reshape(4 * SEG, 128)] + [st[d, 6:7] for d in range(8)], 0
+    ).T
+
     for h in range(heads):
         low, high = window(h)
         cut = slice(h * HDIM, (h + 1) * HDIM)
-        near = e_scr[h]
-        ds = (near * (dp_scr[h] - delta_rows[h])).astype(bf16)
-        dp_far = mm(v_sl[:, low:high], zero_extended(gt, h))
-        ds_far = (parts_far[h] * (dp_far - delta_rows[h])).astype(bf16)
-        dq_ref[cut, :] = (mm(kt[cut], ds) + mm(k_st[cut], ds_far)) * factor
-        dk_ref[cut, :] = mm(qt[cut], ds, NT)
-        dv_ref[cut, :] = mm(gt[cut], near.astype(bf16), NT)
-        far_s.append(mm(q_sl[:, low:high], zero_extended(kt, h)) * factor2)
-        far_p.append(mm(g_sl[:, low:high], zero_extended(vt, h)))
-
+        qz, gz = zero_extended(qt, h), zero_extended(gt, h)
+        qfz, gfz = zero_extended(q_ft, h), zero_extended(g_ft, h)
+        wanted = jnp.where(key_slot < 4, off[5][h], jnp.where(key_slot < 6, off[6][h], off[7][h]))
+        wanted = jnp.where(key_slot == 7, -1, wanted)
+        far = mm(k_far[:, low:high], qz) * factor2
+        far = jnp.where(lane_ok & (lane_rest == wanted), far, NEG)
+        dp_far = mm(v_far[:, low:high], gz)
+        top = jnp.maximum(tops[h], jnp.max(far, axis=0, keepdims=True))
+        e_far = jnp.exp2(far - top)
+        shrink = jnp.exp2(tops[h] - top)
+        total = sums[h] * shrink + jnp.sum(e_far, axis=0, keepdims=True)
+        inv = 1.0 / total
+        delta = (dots[h] * shrink + jnp.sum(e_far * dp_far, axis=0, keepdims=True)) * inv
+        near = e_scr[h] * (shrink * inv)
+        e_far = e_far * inv
+        near_low, far_low = near.astype(bf16), e_far.astype(bf16)
+        ds = (near * (dp_scr[h] - delta)).astype(bf16)
+        ds_far = (e_far * (dp_far - delta)).astype(bf16)
+        att_ref[cut, :] = mm(vt[cut], near_low) + mm(v_ft[cut], far_low)
+        dq_ref[cut, :] = (mm(kt[cut], ds) + mm(k_ft[cut], ds_far)) * factor
+        spot = jnp.where(
+            slot_b < 4,
+            slot_b * 32 + off[5][h],
+            jnp.where(slot_b < 6, (slot_b - 4) * 64 + off[6][h], off[7][h]),
+        )
+        meets = pair_ok & ((spot & key_span[:, :query_n]) == wanted[:, :query_n])
+        other = jnp.where(meets, mm(k_far[:, low:high], qfz) * factor2, NEG)
+        dp_other = mm(v_far[:, low:high], gfz)
+        near_top = notes[h : h + 1]
+        top = jnp.maximum(near_top, jnp.max(other, axis=0, keepdims=True))
+        e_other = jnp.exp2(other - top)
+        shrink = jnp.exp2(near_top - top)
+        total = notes[heads + h : heads + h + 1] * shrink + jnp.sum(
+            e_other, axis=0, keepdims=True
+        )
+        delta = (
+            notes[2 * heads + h : 2 * heads + h + 1] * shrink
+            + jnp.sum(e_other * dp_other, axis=0, keepdims=True)
+        ) / total
+        lse = top + jnp.log2(total)
+        wanted_c = jnp.where(slot_c < 4, off[5][h], jnp.where(slot_c < 6, off[6][h], off[7][h]))
+        score = mm(k_ref[:, low:high], qfz) * factor2
+        prob = jnp.exp2(jnp.where(ok_c & (rest_c == wanted_c), score - lse, NEG))
+        ds_own = (prob * (mm(v_ref[:, low:high], gfz) - delta)).astype(bf16)
+        dk_ref[cut, :] = (mm(qt[cut], ds, NT) + mm(q_ft[cut], ds_own, NT)) * factor
+        dv_ref[cut, :] = mm(gt[cut], near_low, NT) + mm(g_ft[cut], prob.astype(bf16), NT)
     att_out[...] = flipped(att_ref[...])
     dq_out[...] = flipped(dq_ref[...])
-    for copy in second:
-        copy.wait()
-    for d in range(2):
-        slots[4 * d : 4 * d + 4, 0:128] = stat[d, 0:4]
-    for d in range(4):
-        slots[8 + 2 * d : 10 + 2 * d, 0:128] = stat[d, 4:6]
-    for d in range(8):
-        slots[16 + d : 17 + d, 0:128] = stat[d, 6:7]
-    notes = slots[:, 0:128]
-    for h in range(heads):
-        cut = slice(h * HDIM, (h + 1) * HDIM)
-        lse = notes[:, h : h + 1]
-        delta = notes[:, heads + h : heads + h + 1]
-        prob = jnp.exp2(jnp.where(held[h], far_s[h] - lse, NEG))
-        ds = (prob * (far_p[h] - delta)).astype(bf16)
-        dk_ref[cut, :] = (dk_ref[cut, :] + mm(q_st[cut], ds)) * factor
-        dv_ref[cut, :] = dv_ref[cut, :] + mm(g_st[cut], prob.astype(bf16))
     dk_out[...] = flipped(dk_ref[...])
     dv_out[...] = flipped(dv_ref[...])
 
@@ -577,16 +595,12 @@
             *[pltpu.VMEM((rows, width), jnp.bfloat16)] * 4,
             *[pltpu.VMEM((width, rows), jnp.float32)] * 4,
             dma((5,)),
-            pltpu.VMEM((2, 16, width), jnp.bfloat16),
+            pltpu.VMEM((8, 16, width), jnp.bfloat16),
             pltpu.VMEM((4, 16, width), jnp.bfloat16),
-            pltpu.VMEM((8, 16, 128), jnp.bfloat16),
             pltpu.VMEM((8, SEG, 128), jnp.float32),
-            pltpu.VMEM((48, width), jnp.float32),
-            pltpu.VMEM((32, width), jnp.float32),
             pltpu.VMEM((heads, rows, rows), jnp.float32),
             pltpu.VMEM((heads, rows, rows), jnp.float32),
-            dma((2,)), dma((2,)), dma((4,)), dma((4,)),
-            dma((8,)), dma((8,)), dma((8,)), dma((8,)),
+            dma((8,)), dma((8,)), dma((4,)), dma((4,)), dma((8,)), dma((8,)),
         ],
         compiler_params=pltpu.CompilerParams(
             collective_id=0, has_side_effects=True, vmem_limit_bytes=62 * 2**20

time: 20.2 us -> 18.4 us (0.911)
  Pallas kernels: 19.4 us -> 17.6 us
    pallas_call x1, Pallas kernels: 17.6 us -> 15.7 us  [small_body(): pl.pallas_call(functools.partial(kernel, seq_count, heads), out_shape=[ja...]
where the time goes in v2:
time: 18.4 us; the launch traced here: 18.2 us
  Pallas kernels  17.6 us (96%)
  between operations  0.64 us (3%)
    pallas_call x1, Pallas kernels, small_body(): pl.pallas_call(functools.partial(kernel, seq_count, heads), out_shape=[ja...  15.7 us
    pallas_call x1, Pallas kernels, small_body(): pl.pallas_call(write_out, out_shape=[jax.ShapeDtypeStruct((rows, width),...  1.81 us

profile of v2, /device:TPU:0, one launch (start us, length us, event | category | flops | bytes accessed | tf_op | source)
XLA Modules:
  0.0 18.2 jit_solution(3227702048726123614)
XLA Ops:
  0.6 15.7 %shard_map.84 = (bf16[128,384]{1,0:T(8,128)(2,1)}, bf16[128,384]{1,0:T(8,128)(2,1)}, bf16[128,384]{1,0:T(8,128)(2,1)}, bf16[128,384]{1,0:T(8,128)(2,1)}) custom-call(s32[8,16]{1,0:T(8,128)} %offs_hbm.1, bf16[128,384]{1,0:T(8,128)(2,1)} %q_hbm.1, bf16[128,384]{1,0:T(8,128)(2,1)} %k_hbm.1, bf16[128,384]{1,0:T(8,128)(2,1)} %v_hbm.1, bf16[128,384]{1,0:T(8,128)(2,1)} %g_hbm.1), custom_call_target="tpu_custom_call" | custom-call | tf_op jit(solution)/shard_map/pallas_call | solution.py:588
  16.4 1.8 %shard_map.85 = (bf16[128,384]{1,0:T(8,128)(2,1)}, bf16[128,384]{1,0:T(8,128)(2,1)}, bf16[128,384]{1,0:T(8,128)(2,1)}, bf16[128,384]{1,0:T(8,128)(2,1)}) custom-call(bf16[128,384]{1,0:T(8,128)(2,1)} %get-tuple-element.8.refs_0_, bf16[128,384]{1,0:T(8,128)(2,1)} %get-tuple-element.9.refs_1_, bf16[128,384]{1,0:T(8,128)(2,1)} %get-tuple-element.10.refs_2_, ...), custom_call_target="tpu_custom_call" | custom-call | tf_op jit(solution)/shard_map/pallas_call | solution.py:609

commit v3 on v2

--- a/solution.py
+++ b/solution.py
@@ -324,7 +324,7 @@
     seq_count, heads, offs_hbm, q_hbm, k_hbm, v_hbm, g_hbm,
     att_out, dq_out, dk_out, dv_out,
     offs, q_ref, k_ref, v_ref, g_ref, att_ref, dq_ref, dk_ref, dv_ref, fetch,
-    buf_kv, buf_qg, stat, e_scr, dp_scr,
+    buf_kv, buf_qg, stat, e_scr, dp_scr, far_bias, other_bias, own_bias,
     send_kv, recv_kv, send_qg, recv_qg, send_st, recv_st,
 ):
     me = lax.axis_index("seq")
@@ -451,6 +451,8 @@
         dp = mm(v_ref[:, low:high], zero_extended(gt, h))
         e_scr[h] = near
         dp_scr[h] = dp
+        cut = slice(h * HDIM, (h + 1) * HDIM)
+        att_ref[cut, :] = mm(vt[cut], near.astype(bf16))
         total = jnp.sum(near, axis=0, keepdims=True)
         dot = jnp.sum(near * dp, axis=0, keepdims=True)
         tops.append(top)
@@ -490,6 +492,20 @@
     own_pos = lax.broadcasted_iota(jnp.int32, (rows, query_n), 0)
     rest_c = own_pos & span_c
     ok_c = ((dist_c >> reach_c) == 0) & (slot_c != 7) & ((number_c < 32) | (dist_c >= 4))
+
+    for h in range(heads):
+        wanted = jnp.where(key_slot < 4, off[5][h], jnp.where(key_slot < 6, off[6][h], off[7][h]))
+        wanted = jnp.where(key_slot == 7, -1, wanted)
+        far_bias[h] = jnp.where(lane_ok & (lane_rest == wanted), 0.0, NEG)
+        spot = jnp.where(
+            slot_b < 4,
+            slot_b * 32 + off[5][h],
+            jnp.where(slot_b < 6, (slot_b - 4) * 64 + off[6][h], off[7][h]),
+        )
+        meets = pair_ok & ((spot & key_span[:, :query_n]) == wanted[:, :query_n])
+        other_bias[h] = jnp.where(meets, 0.0, NEG)
+        wanted_c = jnp.where(slot_c < 4, off[5][h], jnp.where(slot_c < 6, off[6][h], off[7][h]))
+        own_bias[h] = jnp.where(ok_c & (rest_c == wanted_c), 0.0, NEG)
 
     for copy in first:
         copy.wait()
@@ -507,62 +523,64 @@
     k_ft, v_ft, q_ft, g_ft = [
         x.T.astype(bf16) for x in (k_far32, v_far32, q_far32, g_far32)
     ]
+    cuts = [slice(h * HDIM, (h + 1) * HDIM) for h in range(heads)]
+    far_s, far_dp, oth_s, oth_dp, own_s, own_dp = [], [], [], [], [], []
+    for h in range(heads):
+        low, high = window(h)
+        qz, gz = zero_extended(qt, h), zero_extended(gt, h)
+        qfz, gfz = zero_extended(q_ft, h), zero_extended(g_ft, h)
+        far_s.append(mm(k_far[:, low:high], qz) * factor2 + far_bias[h])
+        far_dp.append(mm(v_far[:, low:high], gz))
+        oth_s.append(mm(k_far[:, low:high], qfz) * factor2 + other_bias[h])
+        oth_dp.append(mm(v_far[:, low:high], gfz))
+        own_s.append(mm(k_ref[:, low:high], qfz) * factor2 + own_bias[h])
+        own_dp.append(mm(v_ref[:, low:high], gfz))
+    near_low, near_ds, far_low, far_ds = [], [], [], []
+    for h in range(heads):
+        top = jnp.maximum(tops[h], jnp.max(far_s[h], axis=0, keepdims=True))
+        e_far = jnp.exp2(far_s[h] - top)
+        shrink = jnp.exp2(tops[h] - top)
+        total = sums[h] * shrink + jnp.sum(e_far, axis=0, keepdims=True)
+        inv = 1.0 / total
+        delta = (dots[h] * shrink + jnp.sum(e_far * far_dp[h], axis=0, keepdims=True)) * inv
+        scale = shrink * inv
+        near = e_scr[h] * scale
+        e_far = e_far * inv
+        near_low.append(near.astype(bf16))
+        far_low.append(e_far.astype(bf16))
+        near_ds.append((near * (dp_scr[h] - delta)).astype(bf16))
+        far_ds.append((e_far * (far_dp[h] - delta)).astype(bf16))
+        att_ref[cuts[h], :] = att_ref[cuts[h], :] * scale
+    for h, cut in enumerate(cuts):
+        att_ref[cut, :] += mm(v_ft[cut], far_low[h])
+        dq_ref[cut, :] = (mm(kt[cut], near_ds[h]) + mm(k_ft[cut], far_ds[h])) * factor
+        dk_ref[cut, :] = mm(qt[cut], near_ds[h], NT)
+        dv_ref[cut, :] = mm(gt[cut], near_low[h], NT)
     for copy in second:
         copy.wait()
     st = stat[...]
     notes = jnp.concatenate(
         [st[0:4].reshape(4 * SEG, 128)] + [st[d, 6:7] for d in range(8)], 0
     ).T
-
+    own_low, own_ds = [], []
     for h in range(heads):
-        low, high = window(h)
-        cut = slice(h * HDIM, (h + 1) * HDIM)
-        qz, gz = zero_extended(qt, h), zero_extended(gt, h)
-        qfz, gfz = zero_extended(q_ft, h), zero_extended(g_ft, h)
-        wanted = jnp.where(key_slot < 4, off[5][h], jnp.where(key_slot < 6, off[6][h], off[7][h]))
-        wanted = jnp.where(key_slot == 7, -1, wanted)
-        far = mm(k_far[:, low:high], qz) * factor2
-        far = jnp.where(lane_ok & (lane_rest == wanted), far, NEG)
-        dp_far = mm(v_far[:, low:high], gz)
-        top = jnp.maximum(tops[h], jnp.max(far, axis=0, keepdims=True))
-        e_far = jnp.exp2(far - top)
-        shrink = jnp.exp2(tops[h] - top)
-        total = sums[h] * shrink + jnp.sum(e_far, axis=0, keepdims=True)
-        inv = 1.0 / total
-        delta = (dots[h] * shrink + jnp.sum(e_far * dp_far, axis=0, keepdims=True)) * inv
-        near = e_scr[h] * (shrink * inv)
-        e_far = e_far * inv
-        near_low, far_low = near.astype(bf16), e_far.astype(bf16)
-        ds = (near * (dp_scr[h] - delta)).astype(bf16)
-        ds_far = (e_far * (dp_far - delta)).astype(bf16)
-        att_ref[cut, :] = mm(vt[cut], near_low) + mm(v_ft[cut], far_low)
-        dq_ref[cut, :] = (mm(kt[cut], ds) + mm(k_ft[cut], ds_far)) * factor
-        spot = jnp.where(
-            slot_b < 4,
-            slot_b * 32 + off[5][h],
-            jnp.where(slot_b < 6, (slot_b - 4) * 64 + off[6][h], off[7][h]),
-        )
-        meets = pair_ok & ((spot & key_span[:, :query_n]) == wanted[:, :query_n])
-        other = jnp.where(meets, mm(k_far[:, low:high], qfz) * factor2, NEG)
-        dp_other = mm(v_far[:, low:high], gfz)
         near_top = notes[h : h + 1]
-        top = jnp.maximum(near_top, jnp.max(other, axis=0, keepdims=True))
-        e_other = jnp.exp2(other - top)
+        top = jnp.maximum(near_top, jnp.max(oth_s[h], axis=0, keepdims=True))
+        e_other = jnp.exp2(oth_s[h] - top)
         shrink = jnp.exp2(near_top - top)
         total = notes[heads + h : heads + h + 1] * shrink + jnp.sum(
             e_other, axis=0, keepdims=True
         )
         delta = (
             notes[2 * heads + h : 2 * heads + h + 1] * shrink
-            + jnp.sum(e_other * dp_other, axis=0, keepdims=True)
+            + jnp.sum(e_other * oth_dp[h], axis=0, keepdims=True)
         ) / total
-        lse = top + jnp.log2(total)
-        wanted_c = jnp.where(slot_c < 4, off[5][h], jnp.where(slot_c < 6, off[6][h], off[7][h]))
-        score = mm(k_ref[:, low:high], qfz) * factor2
-        prob = jnp.exp2(jnp.where(ok_c & (rest_c == wanted_c), score - lse, NEG))
-        ds_own = (prob * (mm(v_ref[:, low:high], gfz) - delta)).astype(bf16)
-        dk_ref[cut, :] = (mm(qt[cut], ds, NT) + mm(q_ft[cut], ds_own, NT)) * factor
-        dv_ref[cut, :] = mm(gt[cut], near_low, NT) + mm(g_ft[cut], prob.astype(bf16), NT)
+        prob = jnp.exp2(own_s[h] - (top + jnp.log2(total)))
+        own_low.append(prob.astype(bf16))
+        own_ds.append((prob * (own_dp[h] - delta)).astype(bf16))
+    for h, cut in enumerate(cuts):
+        dk_ref[cut, :] = (dk_ref[cut, :] + mm(q_ft[cut], own_ds[h], NT)) * factor
+        dv_ref[cut, :] += mm(g_ft[cut], own_low[h], NT)
     att_out[...] = flipped(att_ref[...])
     dq_out[...] = flipped(dq_ref[...])
     dk_out[...] = flipped(dk_ref[...])
@@ -600,6 +618,9 @@
             pltpu.VMEM((8, SEG, 128), jnp.float32),
             pltpu.VMEM((heads, rows, rows), jnp.float32),
             pltpu.VMEM((heads, rows, rows), jnp.float32),
+            pltpu.VMEM((heads, 8 * SEG, rows), jnp.float32),
+            pltpu.VMEM((heads, 8 * SEG, 5 * SEG), jnp.float32),
+            pltpu.VMEM((heads, rows, 5 * SEG), jnp.float32),
             dma((8,)), dma((8,)), dma((4,)), dma((4,)), dma((8,)), dma((8,)),
         ],
         compiler_params=pltpu.CompilerParams(

time: 18.4 us -> 15.1 us (0.82)
  Pallas kernels: 17.6 us -> 14.2 us
    pallas_call x1, Pallas kernels: 15.7 us -> 12.4 us  [small_body(): pl.pallas_call(functools.partial(kernel, seq_count, heads), out_shape=[ja...]
where the time goes in v3:
time: 15.1 us; the launch traced here: 14.9 us
  Pallas kernels  14.2 us (94%)
  between operations  0.64 us (4%)
    pallas_call x1, Pallas kernels, small_body(): pl.pallas_call(functools.partial(kernel, seq_count, heads), out_shape=[ja...  12.4 us
    pallas_call x1, Pallas kernels, small_body(): pl.pallas_call(write_out, out_shape=[jax.ShapeDtypeStruct((rows, width),...  1.81 us

profile of v3, /device:TPU:0, one launch (start us, length us, event | category | flops | bytes accessed | tf_op | source)
XLA Modules:
  0.0 14.9 jit_solution(7264772119195045035)
XLA Ops:
  0.6 12.4 %shard_map.84 = (bf16[128,384]{1,0:T(8,128)(2,1)}, bf16[128,384]{1,0:T(8,128)(2,1)}, bf16[128,384]{1,0:T(8,128)(2,1)}, bf16[128,384]{1,0:T(8,128)(2,1)}) custom-call(s32[8,16]{1,0:T(8,128)} %offs_hbm.1, bf16[128,384]{1,0:T(8,128)(2,1)} %q_hbm.1, bf16[128,384]{1,0:T(8,128)(2,1)} %k_hbm.1, bf16[128,384]{1,0:T(8,128)(2,1)} %v_hbm.1, bf16[128,384]{1,0:T(8,128)(2,1)} %g_hbm.1), custom_call_target="tpu_custom_call" | custom-call | tf_op jit(solution)/shard_map/pallas_call | solution.py:606
  13.1 1.8 %shard_map.85 = (bf16[128,384]{1,0:T(8,128)(2,1)}, bf16[128,384]{1,0:T(8,128)(2,1)}, bf16[128,384]{1,0:T(8,128)(2,1)}, bf16[128,384]{1,0:T(8,128)(2,1)}) custom-call(bf16[128,384]{1,0:T(8,128)(2,1)} %get-tuple-element.8.refs_0_, bf16[128,384]{1,0:T(8,128)(2,1)} %get-tuple-element.9.refs_1_, bf16[128,384]{1,0:T(8,128)(2,1)} %get-tuple-element.10.refs_2_, ...), custom_call_target="tpu_custom_call" | custom-call | tf_op jit(solution)/shard_map/pallas_call | solution.py:630

commit v4 on v3

--- a/solution.py
+++ b/solution.py
@@ -324,6 +324,7 @@
     seq_count, heads, offs_hbm, q_hbm, k_hbm, v_hbm, g_hbm,
     att_out, dq_out, dk_out, dv_out,
     offs, q_ref, k_ref, v_ref, g_ref, att_ref, dq_ref, dk_ref, dv_ref, fetch,
+    att_low, dq_low, dk_low, dv_low, left,
     buf_kv, buf_qg, stat, e_scr, dp_scr, far_bias, other_bias, own_bias,
     send_kv, recv_kv, send_qg, recv_qg, send_st, recv_st,
 ):
@@ -336,6 +337,12 @@
     ]
     for copy in fetches:
         copy.start()
+    leave = [
+        pltpu.make_async_copy(here, there, left.at[i])
+        for i, (here, there) in enumerate(
+            ((att_low, att_out), (dq_low, dq_out), (dk_low, dk_out), (dv_low, dv_out))
+        )
+    ]
     f32, bf16 = jnp.float32, jnp.bfloat16
     factor = HDIM ** (-0.5)
     factor2 = factor * math.log2(math.e)
@@ -436,6 +443,7 @@
     lane8 = lax.broadcasted_iota(jnp.int32, (SEG, 128), 1)
     row8 = lax.broadcasted_iota(jnp.int32, (SEG, 128), 0)
     note = jnp.where((row8 == SEG - 1) & (lane8 >= heads) & (lane8 < 2 * heads), 1.0, 0.0)
+    scores, counts, dps = [], [], []
     for h in range(heads):
         low, high = window(h)
         before = 32 * (h % 4)
@@ -443,22 +451,20 @@
         parts.append(feats[h].astype(bf16))
         if before < 96:
             parts.append(jnp.zeros((96 - before, rows), bf16))
-        count = mm(feat_rows[h // 4], jnp.concatenate(parts, 0))
-        score = mm(k_ref[:, low:high], zero_extended(qt, h)) * factor2
-        score = jnp.where(count > 0, score, NEG)
+        counts.append(mm(feat_rows[h // 4], jnp.concatenate(parts, 0)))
+        scores.append(mm(k_ref[:, low:high], zero_extended(qt, h)) * factor2)
+        dps.append(mm(v_ref[:, low:high], zero_extended(gt, h)))
+    for h in range(heads):
+        score = jnp.where(counts[h] > 0, scores[h], NEG)
         top = jnp.max(score, axis=0, keepdims=True)
-        near = count * jnp.exp2(score - top)
-        dp = mm(v_ref[:, low:high], zero_extended(gt, h))
+        near = counts[h] * jnp.exp2(score - top)
         e_scr[h] = near
-        dp_scr[h] = dp
-        cut = slice(h * HDIM, (h + 1) * HDIM)
-        att_ref[cut, :] = mm(vt[cut], near.astype(bf16))
-        total = jnp.sum(near, axis=0, keepdims=True)
-        dot = jnp.sum(near * dp, axis=0, keepdims=True)
+        dp_scr[h] = dps[h]
         tops.append(top)
-        sums.append(total)
-        dots.append(dot)
-        for kind, row in enumerate((top, total, dot)):
+        sums.append(jnp.sum(near, axis=0, keepdims=True))
+        dots.append(jnp.sum(near * dps[h], axis=0, keepdims=True))
+    for h in range(heads):
+        for kind, row in enumerate((tops[h], sums[h], dots[h])):
             column = jnp.sum(jnp.where(picks[h], row, 0.0), axis=1, keepdims=True)
             here = (lane8 == kind * heads + h) & (row8 < SEG - 1)
             note = jnp.where(here, column, note)
@@ -466,6 +472,10 @@
     second = [remote(stat, send_st, recv_st, d) for d in (7, 6, 5, 4, 3, 2, 1)]
     for copy in second:
         copy.start()
+
+    for h in range(heads):
+        cut = slice(h * HDIM, (h + 1) * HDIM)
+        att_ref[cut, :] = mm(vt[cut], e_scr[h].astype(bf16))
 
     far_n = SEG * seq_count
     query_n = 5 * SEG
@@ -556,6 +566,10 @@
         dq_ref[cut, :] = (mm(kt[cut], near_ds[h]) + mm(k_ft[cut], far_ds[h])) * factor
         dk_ref[cut, :] = mm(qt[cut], near_ds[h], NT)
         dv_ref[cut, :] = mm(gt[cut], near_low[h], NT)
+    att_low[...] = flipped(att_ref[...])
+    leave[0].start()
+    dq_low[...] = flipped(dq_ref[...])
+    leave[1].start()
     for copy in second:
         copy.wait()
     st = stat[...]
@@ -581,10 +595,12 @@
     for h, cut in enumerate(cuts):
         dk_ref[cut, :] = (dk_ref[cut, :] + mm(q_ft[cut], own_ds[h], NT)) * factor
         dv_ref[cut, :] += mm(g_ft[cut], own_low[h], NT)
-    att_out[...] = flipped(att_ref[...])
-    dq_out[...] = flipped(dq_ref[...])
-    dk_out[...] = flipped(dk_ref[...])
-    dv_out[...] = flipped(dv_ref[...])
+    dk_low[...] = flipped(dk_ref[...])
+    leave[2].start()
+    dv_low[...] = flipped(dv_ref[...])
+    leave[3].start()
+    for copy in leave:
+        copy.wait()
 
 
 def write_out(*refs):
@@ -601,18 +617,19 @@
     heads = width // HDIM
     seq_count = lax.axis_size("seq")
     hbm = pl.BlockSpec(memory_space=pltpu.HBM)
-    vmem = pl.BlockSpec(memory_space=pltpu.VMEM)
     dma = pltpu.SemaphoreType.DMA
     outs = pl.pallas_call(
         functools.partial(kernel, seq_count, heads),
         out_shape=[jax.ShapeDtypeStruct((rows, width), jnp.bfloat16)] * 4,
         in_specs=[hbm] * 5,
-        out_specs=[vmem] * 4,
+        out_specs=[hbm] * 4,
         scratch_shapes=[
             pltpu.SMEM(offsets.shape, jnp.int32),
             *[pltpu.VMEM((rows, width), jnp.bfloat16)] * 4,
             *[pltpu.VMEM((width, rows), jnp.float32)] * 4,
             dma((5,)),
+            *[pltpu.VMEM((rows, width), jnp.bfloat16)] * 4,
+            dma((4,)),
             pltpu.VMEM((8, 16, width), jnp.bfloat16),
             pltpu.VMEM((4, 16, width), jnp.bfloat16),
             pltpu.VMEM((8, SEG, 128), jnp.float32),
@@ -630,7 +647,7 @@
     return pl.pallas_call(
         write_out,
         out_shape=[jax.ShapeDtypeStruct((rows, width), jnp.bfloat16)] * 4,
-        in_specs=[vmem] * 4,
+        in_specs=[hbm] * 4,
         out_specs=[hbm] * 4,
         scratch_shapes=[dma((4,))],
     )(*outs)

time: 15.1 us -> 26.3 us (1.74)
  Pallas kernels: 14.2 us -> 25.5 us
    pallas_call x1, Pallas kernels: 1.81 us -> 13.1 us  [small_body(): pl.pallas_call(write_out, out_shape=[jax.ShapeDtypeStruct((rows, width),...]
where the time goes in v4:
time: 26.3 us; the launch traced here: 26.1 us
  Pallas kernels  25.5 us (97%)
  between operations  0.64 us (2%)
    pallas_call x1, Pallas kernels, small_body(): pl.pallas_call(write_out, out_shape=[jax.ShapeDtypeStruct((rows, width),...  13.1 us
    pallas_call x1, Pallas kernels, small_body(): pl.pallas_call(functools.partial(kernel, seq_count, heads), out_shape=[ja...  12.4 us

profile of v4, /device:TPU:0, one launch (start us, length us, event | category | flops | bytes accessed | tf_op | source)
XLA Modules:
  0.0 26.1 jit_solution(16577685304522133658)
XLA Ops:
  0.6 12.4 %shard_map.84 = (bf16[128,384]{1,0:T(8,128)(2,1)}, bf16[128,384]{1,0:T(8,128)(2,1)}, bf16[128,384]{1,0:T(8,128)(2,1)}, bf16[128,384]{1,0:T(8,128)(2,1)}) custom-call(s32[8,16]{1,0:T(8,128)} %offs_hbm.1, bf16[128,384]{1,0:T(8,128)(2,1)} %q_hbm.1, bf16[128,384]{1,0:T(8,128)(2,1)} %k_hbm.1, bf16[128,384]{1,0:T(8,128)(2,1)} %v_hbm.1, bf16[128,384]{1,0:T(8,128)(2,1)} %g_hbm.1), custom_call_target="tpu_custom_call" | custom-call | tf_op jit(solution)/shard_map/pallas_call | solution.py:621
  13.1 13.1 %shard_map.85 = (bf16[128,384]{1,0:T(8,128)(2,1)}, bf16[128,384]{1,0:T(8,128)(2,1)}, bf16[128,384]{1,0:T(8,128)(2,1)}, bf16[128,384]{1,0:T(8,128)(2,1)}) custom-call(bf16[128,384]{1,0:T(8,128)(2,1)} %get-tuple-element.8.refs_0_, bf16[128,384]{1,0:T(8,128)(2,1)} %get-tuple-element.9.refs_1_, bf16[128,384]{1,0:T(8,128)(2,1)} %get-tuple-element.10.refs_2_, ...), custom_call_target="tpu_custom_call" | custom-call | tf_op jit(solution)/shard_map/pallas_call | solution.py:647
